TPU v7x, 512 devices: a whole 4x8x8 slice. The times are simulated.
512 devices in a mesh: bld: 128 (over z, y, core), real: 4 (over x).
Axes of the slice: x: 4, y: 8, z: 8, core: 2. Of those that a mesh axis runs over, the one named last changes fastest.
Arguments:
- site_ln: float32 [64, 16384], P('real', 'bld'), may hold values from -4 to 4
- site_of: int32 [16384], P('bld'), may hold values from 0 to 16383
- county_of: int32 [16384], P('bld'), may hold values from 0 to 15
- tract_of: int32 [16384], P('bld'), may hold values from 0 to 2047
- comp_type: int32 [24, 16384], P(None, 'bld'), may hold values from 0 to 255
- comp_qty: int32 [24, 16384], P(None, 'bld'), may hold values from 0 to 12, as said below
- amplify: float32 [24, 16384], P(None, 'bld'), may hold values from -1.5 to 1.5
- frag_median: float32 [256], replicated, may hold values from -1 to 1
- frag_step: float32 [256], replicated, may hold values from 0.3 to 1
- frag_beta: float32 [256], replicated, may hold values from 0.4 to 0.8
- state_cost: float32 [3, 256], replicated, may hold values from 0.0005 to 0.008
Outputs:
- tract_loss: float32 [2048, 64], P('bld', 'real')
- tract_avg: float32 [2048], P('bld')
Inputs may be any that keep to these rules, and one draw needn't show every extreme that they name: `comp_qty`: the quantities tend to grow with the building's index.
All inputs are finite; a program needn't handle non-finite values.
Results may differ from a plain program's by a relative error of at most 0.00036.
Values may be sent and summed in bfloat16 or wider, within the bound.
A program may use at most 64 MiB of HBM per device.

v0:
```python
import jax
import jax.numpy as jnp
from jax import lax
from jax.sharding import PartitionSpec as P

STATES = 3
COUNTIES = 16
TRACT_DEV = 16


surge_peak = 1.0
root_half = 0.7071067811865476
highest = lax.Precision.HIGHEST


def normal_cdf(value):
    return 0.5 * (1.0 + lax.erf(value * root_half))


def shards(
    site_ln,
    site_of,
    county_of,
    tract_of,
    comp_type,
    comp_qty,
    amplify,
    frag_median,
    frag_step,
    frag_beta,
    state_cost,
):
    real_count = site_ln.shape[0]
    bld_count = site_of.shape[0]
    group_count = comp_type.shape[0]
    type_count = frag_median.shape[0]
    blocks_bld = lax.axis_size("bld")
    key_count = COUNTIES * type_count
    block_part = lax.all_gather(site_ln, "bld", axis=1, tiled=True)
    width = block_part.shape[1]
    matches = (site_of[None, :] == jnp.arange(width, dtype=jnp.int32)[:, None]).astype(jnp.float32)
    log_intensity = jnp.dot(
        block_part, matches, precision=highest, preferred_element_type=jnp.float32
    )
    frag_table = jnp.concatenate(
        [frag_median[None], frag_step[None], frag_beta[None], state_cost], axis=0
    )
    chosen = (
        jnp.arange(type_count, dtype=jnp.int32)[:, None] == comp_type.reshape(-1)[None, :]
    ).astype(jnp.float32)
    type_param = jnp.dot(frag_table, chosen, precision=highest, preferred_element_type=jnp.float32)
    type_param = type_param.reshape(frag_table.shape[0], group_count, bld_count)
    demand = log_intensity[None, :, :] + amplify[:, None, :]
    medians = type_param[0][:, None, :]
    spacing = type_param[1][:, None, :]
    spread = type_param[2][:, None, :]
    expect = jnp.zeros_like(demand)
    cost_prev = jnp.zeros_like(medians)
    damaged_p = demand
    for damage_lvl in range(STATES):
        chance = normal_cdf((demand - medians - damage_lvl * spacing) / spread)
        cost_now = type_param[3 + damage_lvl][:, None, :]
        expect = expect + chance * (cost_now - cost_prev)
        cost_prev = cost_now
        if damage_lvl == 0:
            damaged_p = chance
    quantity = comp_qty.astype(jnp.float32)
    damaged = (quantity[:, None, :] * damaged_p).astype(jnp.bfloat16)
    key_ids = county_of[None, :] * type_count + comp_type
    key_iota = jnp.arange(key_count, dtype=jnp.int32)

    def collect(group_at, running):
        group_keys = lax.dynamic_index_in_dim(key_ids, group_at, 0, keepdims=False)
        matches = (group_keys[:, None] == key_iota[None, :]).astype(jnp.bfloat16)
        group_part = lax.dynamic_index_in_dim(damaged, group_at, 0, keepdims=False)
        return running + jnp.dot(group_part, matches, preferred_element_type=jnp.float32)

    county = lax.fori_loop(0, group_count, collect, jnp.zeros((real_count, key_count), jnp.float32))
    half_point = float(4 * bld_count * blocks_bld * group_count // key_count + 1)
    county_all = lax.psum(county, "bld")
    surge_cost = (1.0 + surge_peak * county_all / (county_all + half_point)).astype(jnp.bfloat16)

    def apply_surge(group_at, running):
        group_keys = lax.dynamic_index_in_dim(key_ids, group_at, 0, keepdims=False)
        matches = (group_keys[:, None] == key_iota[None, :]).astype(jnp.bfloat16)
        lookup = lax.dot_general(
            surge_cost, matches, (((1,), (1,)), ((), ())), preferred_element_type=jnp.float32
        )
        weight = lax.dynamic_index_in_dim(quantity, group_at, 0, keepdims=False)
        group_exp = lax.dynamic_index_in_dim(expect, group_at, 0, keepdims=False)
        return running + weight[None, :] * group_exp * lookup

    bld_loss = lax.fori_loop(
        0, group_count, apply_surge, jnp.zeros((real_count, bld_count), jnp.float32)
    )
    flipped = bld_loss.T
    matches = (
        tract_of[None, :] - 0 == jnp.arange(TRACT_DEV * blocks_bld, dtype=jnp.int32)[:, None]
    ).astype(jnp.float32)
    all_tracts = lax.psum(
        jnp.dot(matches, flipped, precision=highest, preferred_element_type=jnp.float32), "bld"
    )
    own_tracts = lax.dynamic_slice_in_dim(
        all_tracts, lax.axis_index("bld") * TRACT_DEV, TRACT_DEV, 0
    )
    tract_sums = lax.psum(jnp.sum(own_tracts, axis=1), "real")
    tract_avg = tract_sums / (real_count * lax.axis_size("real"))
    return (own_tracts, tract_avg)


def solution(mesh):
    in_specs = (
        P("real", "bld"),
        P("bld"),
        P("bld"),
        P("bld"),
        P(None, "bld"),
        P(None, "bld"),
        P(None, "bld"),
        P(),
        P(),
        P(),
        P(),
    )
    out_specs = (P("bld", "real"), P("bld"))
    return jax.shard_map(shards, mesh=mesh, in_specs=in_specs, out_specs=out_specs, check_vma=False)
```

profile of v0, /device:TPU:1, one launch (start us, length us, event | category | flops | bytes accessed | tf_op | source)
XLA Modules:
  0.0 523.8 jit_solution(13472862224158825418)
XLA Ops:
  7.2 0.7 all-gather.2.cloned.1.call-update
  8.0 0.7 broadcast_multiply_fusion.4
  8.6 0.7 broadcast_add_fusion
  9.3 1.8 fusion.17
  11.2 0.7 broadcast_multiply_fusion.2
  12.0 84.3 %all-gather.2.cloned.1.call-done = f32[16,16384]{1,0:T(8,128)} async-done(((f32[16,128]{1,0:T(8,128)}), f32[16,16384]{1,0:T(8,128)}) %all-gather.2.cloned.1.call-update) | async-done | bytes 1048592 | tf_op jit(solution)/shard_map/all_gather | solution.py:39
  96.2 4.1 fusion.19
  100.5 12.6 %while.28 = (s32[]{:T(128)}, f32[16,4096]{1,0:T(8,128)S(1)}, bf16[24,16,128]{2,1,0:T(8,128)(2,1)S(1)}, s32[24,128]{1,0:T(8,128)S(1)}, s32[]{:T(128)}, /*index=5*/s32[]{:T(128)}) while((s32[]{:T(128)}, f32[16,4096]{1,0:T(8,128)S(1)}, bf16[24,16,128]{2,1,0:T(8,128)(2,1)S(1)}, s32[24,128]{1,0:T(8,128)S(1)}, s32[]{:T(128)}, ...), condition=%wide.region_1.2_spmd.clone, body=%wide.region_0.1_spmd.clone.sunk | while | flops 17432580 | bytes 530007 | solution.py:78
  100.6 0.5 convolution_add_fusion.2
  101.1 0.5 convolution_add_fusion.2
  101.6 0.5 convolution_add_fusion.2
  102.2 0.5 convolution_add_fusion.2
  102.7 0.5 convolution_add_fusion.2
  103.2 0.5 convolution_add_fusion.2
  110.0 0.5 convolution_add_fusion.2
  113.2 0.7 copy-done
  114.0 184.1 %all-reduce.3.cloned.1.call-done = f32[16,4096]{1,0:T(8,128)} async-done(((f32[16,4096]{1,0:T(8,128)}), f32[16,4096]{1,0:T(8,128)}) %all-reduce.3.cloned.1.call-update) | async-done | bytes 262160 | tf_op jit(solution)/shard_map/psum | solution.py:80
  298.1 1.0 fusion.23
  299.1 12.9 %while.29 = (s32[]{:T(128)}, f32[16,128]{1,0:T(8,128)S(1)}, f32[24,128]{1,0:T(8,128)S(1)}, f32[24,16,128]{2,1,0:T(8,128)S(1)}, s32[24,128]{1,0:T(8,128)S(1)}, /*...) while((s32[]{:T(128)}, f32[16,128]{1,0:T(8,128)S(1)}, f32[24,128]{1,0:T(8,128)S(1)}, ...), condition=%wide.region_4.5_spmd.clone, body=%wide.region_3.4_spmd.clone.sunk | while | flops 17309700 | bytes 158827 | solution.py:93
  312.0 1.6 fusion.20
  313.6 193.4 %all-reduce.5.cloned.1.call-done = f32[2048,16]{1,0:T(8,128)} async-done(((f32[2048,16]{1,0:T(8,128)}), f32[2048,16]{1,0:T(8,128)}) %all-reduce.5.cloned.1.call-update) | async-done | bytes 131088 | tf_op jit(solution)/shard_map/psum | solution.py:100
  507.0 1.4 fusion.33
  508.4 8.4 %psum.23 = f32[16]{0:T(128)S(1)} all-reduce(f32[16]{0:T(128)S(1)} %get-tuple-element.282), channel_id=1, replica_groups=mesh['bld'=128,'real'=4] {'real'}, use_global_device_ids=true, to_apply=%region_7.8 | all-reduce | flops 16 | bytes 128 | tf_op jit(solution)/shard_map/psum | solution.py:106
  516.8 0.5 broadcast_multiply_fusion.3
  (130 shorter events, 21.6 us)
Async XLA Ops:
  7.2 89.1 %all-gather.2.cloned.1.call-start = ((), (), s32[]{:S(2)}) async-start(), calls=%async_computation | async-start | bytes 1056768 | tf_op jit(solution)/shard_map/all_gather | solution.py:39
  7.9 290.2 %all-reduce.3.cloned.1.call-start = ((), (), s32[]{:S(2)}) async-start(), calls=%async_computation.1 | async-start | bytes 524288 | tf_op jit(solution)/shard_map/psum | solution.py:80
  12.0 88.4 %copy-start.2 = (f32[24,128]{1,0:T(8,128)S(1)}, f32[24,128]{1,0:T(8,128)}, u32[]{:S(2)}) copy-start(f32[24,128]{1,0:T(8,128)} %param.21) | copy-start | bytes 36868
  100.5 13.4 %copy-start.1 = (s32[24,128]{1,0:T(8,128)S(1)}, s32[24,128]{1,0:T(8,128)}, u32[]{:S(2)}) copy-start(s32[24,128]{1,0:T(8,128)} %param.20) | copy-start | bytes 36868
  113.2 0.7 copy-start
  113.9 393.1 %all-reduce.5.cloned.1.call-start = ((), (), s32[]{:S(2)}) async-start(), calls=%async_computation.2 | async-start | bytes 2097152 | tf_op jit(solution)/shard_map/psum | solution.py:100
  299.1 12.9 %copy-start.3 = (s32[128]{0:T(128)S(1)}, s32[128]{0:T(128)}, u32[]{:S(2)}) copy-start(s32[128]{0:T(128)} %param.18) | copy-start | bytes 1540
Sparse Core Ops, SparseCore 0:
  11.0 85.1 all-gather.1
  114.0 184.0 all-reduce.2
  313.7 193.2 all-reduce.4
where the time goes:
time: 527 us; the launch traced here: 524 us
  waiting for transfers between devices  462 us (88%)
  matrix products  31.7 us (6%)
  between operations  13.8 us (3%)
  blocking collectives  8.4 us (2%)
    psum x1, waiting for transfers between devices, shards(): lax.psum(jnp.dot(matches, flipped, precision=highest, preferred_element_t...  193 us
    psum x1, waiting for transfers between devices, shards(): county_all = lax.psum(county, 'bld')  184 us
    all_gather x1, waiting for transfers between devices, shards(): block_part = lax.all_gather(site_ln, 'bld', axis=1, tiled=True)  84.3 us
    dot_general x24, matrix products, collect(): jnp.dot(group_part, matches, preferred_element_type=jnp.float32)  12.2 us
    dot_general x24, matrix products, apply_surge(): lax.dot_general(surge_cost, matches, (((1,), (1,)), ((), ())), preferred_...  11.9 us
  transfers between devices with their start and end apart: 3, of which 3 were waited for; matrix products, arithmetic and copies ran while one was open for 1% of the time, Pallas kernels for 0%

commit v1 on v0

v1 whole, which is shorter than its diff:
```python
import jax
import jax.numpy as jnp
from jax import lax
from jax.experimental import pallas as pl
from jax.experimental.pallas import tpu as pltpu
from jax.sharding import PartitionSpec as P

LINE = 8
GROUPS = 24
TYPES = 256
COUNTIES = 16
LANES = 128
HALF = 8
WIDE = 2 * LANES
REALS_ALL = 64.0
HALF_POINT = 385.0
ROOT_HALF = 0.7071067811865476
MESH = pl.DeviceIdType.MESH
F32 = jnp.float32
BF16 = jnp.bfloat16
HIGHEST = lax.Precision.HIGHEST
NT = (((1,), (1,)), ((), ()))


def lanes_of(table, index):
    return jnp.take_along_axis(table, index, axis=1, mode="promise_in_bounds")


def drain(ref, sem):
    pltpu.make_async_copy(ref, ref, sem).wait()


def kernel(
    site_ln, site_of, county_of, tract_of, comp_type, comp_qty, amplify,
    frag_median, frag_step, frag_beta, state_cost,
    loss_out, avg_out,
    b_site, b_county, b_tract, b_type, b_qty, b_amp,
    t_med, t_step, t_beta, t_cost,
    sites, p_base, p_inv, p_step, p_half, p_c0, p_c1, p_c2,
    hot, spread, args, weight,
    part, got3, half_sum, got4, surge_own, surge,
    dest, terms, tract_part, got6, rows, got7, row, got8,
    loc_sem, par_sem, bld_send, bld_recv,
    s1, r1, s2, r2, s3, r3, s4, r4, s5, r5, s6, r6, s7, r7, s8, r8,
):
    me = lax.axis_index("bld")
    x = lax.axis_index("real")
    z = me // (2 * LINE)
    y = lax.rem(me // 2, LINE)
    c = lax.rem(me, 2)

    def at(zz, yy, cc):
        return {"bld": (zz * LINE + yy) * 2 + cc}

    def send(src, dst, ssem, rsem, who):
        pltpu.make_async_remote_copy(
            src_ref=src, dst_ref=dst, send_sem=ssem, recv_sem=rsem,
            device_id=who, device_id_type=MESH,
        ).start()

    barrier = pltpu.get_barrier_semaphore()

    def hello(who):
        pl.semaphore_signal(barrier, inc=1, device_id=who, device_id_type=MESH)

    hello(at(z, y, 1 - c))
    for i in range(1, LINE):
        for h in range(2):
            hello(at(z, lax.rem(y + i, LINE), h))
            hello(at(lax.rem(z + i, LINE), y, h))
    for i in range(1, 4):
        hello({"real": lax.rem(x + i, 4)})

    buildings = (
        (site_of, b_site), (county_of, b_county), (tract_of, b_tract),
        (comp_type, b_type), (comp_qty, b_qty), (amplify, b_amp),
    )
    tables = ((frag_median, t_med), (frag_step, t_step), (frag_beta, t_beta), (state_cost, t_cost))
    own = [pltpu.make_async_copy(a, b.at[0], loc_sem.at[n]) for n, (a, b) in enumerate(buildings)]
    own += [pltpu.make_async_copy(a, b, par_sem.at[n]) for n, (a, b) in enumerate(tables)]
    for copy in own:
        copy.start()

    pl.semaphore_wait(barrier, 1 + 4 * (LINE - 1) + 3)

    p = y * (1 - c) + z * c
    q = z * (1 - c) + y * c
    mine = sites.at[c, q, p]
    local = pltpu.make_async_copy(site_ln.at[pl.ds(pl.multiple_of(c * HALF, HALF), HALF)], mine, r1.at[c])
    local.start()
    send(site_ln.at[pl.ds(pl.multiple_of((1 - c) * HALF, HALF), HALF)], mine, s1, r1.at[c], at(z, y, 1 - c))
    for i in range(1, LINE):
        pp = lax.rem(p + i, LINE)
        for h in range(2):
            zz = q * (1 - c) + pp * c
            yy = pp * (1 - c) + q * c
            send(site_ln.at[pl.ds(h * HALF, HALF)], mine, s1, r1.at[c], at(zz, yy, h))
    trade = [
        pltpu.make_async_remote_copy(
            src_ref=a, dst_ref=b.at[1], send_sem=bld_send.at[n], recv_sem=bld_recv.at[n],
            device_id=at(z, y, 1 - c), device_id_type=MESH,
        )
        for n, (a, b) in enumerate(buildings)
    ]
    for copy in trade:
        copy.start()

    drain(sites.at[0, z], r1.at[0])
    for i in range(1, LINE):
        send(sites.at[0, z], sites.at[0, z], s2, r2.at[0, i], at(lax.rem(z + i, LINE), y, c))
    drain(sites.at[1, y], r1.at[1])
    for i in range(1, LINE):
        send(sites.at[1, y], sites.at[1, y], s2, r2.at[1, i], at(z, lax.rem(y + i, LINE), c))

    for copy in own:
        copy.wait()
    for copy in trade:
        copy.wait()
    inv_row = ROOT_HALF / t_beta[...]
    step_row = t_step[...] * inv_row
    med_row = t_med[...]
    cost = t_cost[...]

    def cost_rows(level):
        now = cost[level : level + 1]
        if level:
            now = now - cost[level - 1 : level]
        return now[:, :LANES], now[:, LANES:]

    def pair(table):
        return table[0:1], table[1:2]

    looked = (
        (pair(med_row), p_base), (pair(inv_row), p_inv), (pair(step_row), p_step),
        (cost_rows(0), p_c0), (cost_rows(1), p_c1), (cost_rows(2), p_c2),
    )
    for bh in range(2):
        for g in range(0, GROUPS, 8):
            index = b_type[bh, g : g + 8, :]
            low = index & (LANES - 1)
            high = index >= LANES
            for (first, second), into in looked:
                value = jnp.where(
                    high,
                    lanes_of(jnp.broadcast_to(second, (8, LANES)), low),
                    lanes_of(jnp.broadcast_to(first, (8, LANES)), low),
                )
                if into is p_base:
                    value = b_amp[bh, g : g + 8, :] - value
                into[bh, g : g + 8, :] = value
            p_half[bh, g : g + 8, :] = 0.5 * b_qty[bh, g : g + 8, :].astype(F32)

    one = jnp.ones((16, LANES), BF16)
    zero = jnp.zeros((16, LANES), BF16)
    count = lax.broadcasted_iota(jnp.int32, (16, LANES), 0)

    counts = [(count + 16 * n).astype(F32).astype(BF16) for n in range(TYPES // 16)]

    def make_hot(g, _):
        for bh in range(2):
            types = jnp.broadcast_to(b_type[bh, pl.ds(g, 1), :], (16, LANES)).astype(F32).astype(BF16)
            columns = pl.ds(pl.multiple_of(g * WIDE + bh * LANES, LANES), LANES)
            for n in range(TYPES // 16):
                hot[n * 16 : (n + 1) * 16, columns] = jnp.where(types == counts[n], one, zero)
        return 0

    lax.fori_loop(0, GROUPS, make_hot, 0)

    for bh in range(2):
        owner = b_tract[bh] // 16
        place = (owner & 15) * LINE + owner // 16
        place = jnp.broadcast_to(place, (16, LANES)).astype(F32).astype(BF16)
        for n in range(8):
            value = jnp.where(place == counts[n], one, zero)
            for piece in range(3):
                dest[n * 16 : (n + 1) * 16, piece * WIDE + bh * LANES : piece * WIDE + (bh + 1) * LANES] = value

    upper = (count >= HALF).astype(jnp.int32)

    def pair_masks(ref, bh):
        value = jnp.broadcast_to(ref, (16, LANES)) - upper
        value = value.astype(F32).astype(BF16)
        return [jnp.where(value == jnp.asarray(2 * n, BF16), one, zero) for n in range(8)]

    low = [jnp.broadcast_to(b_site[bh] & (LANES - 1), (HALF, LANES)) for bh in range(2)]
    high = [jnp.broadcast_to(b_site[bh] // LANES, (HALF, LANES)) for bh in range(2)]
    level = [jnp.zeros((HALF, LANES), F32) for _ in range(2)]

    def pick(level, route, line):
        for n in range(LINE):
            tile = sites[route, line, n]
            block = (line * 16 + 2 * n) if route == 0 else (n * 16 + line * 2 + 1)
            level = [jnp.where(high[bh] == block, lanes_of(tile, low[bh]), level[bh]) for bh in range(2)]
        return level

    level = pick(level, 0, z)
    level = pick(level, 1, y)
    for i in (1, 7, 2, 6, 3, 5, 4):
        zz = lax.rem(z + LINE - i, LINE)
        drain(sites.at[0, zz], r2.at[0, i])
        level = pick(level, 0, zz)
        yy = lax.rem(y + LINE - i, LINE)
        drain(sites.at[1, yy], r2.at[1, i])
        level = pick(level, 1, yy)

    for bh in range(2):
        masks = pair_masks(b_county[bh], bh)

        def damage(g, _):
            row_at = pl.ds(g, 1)
            arg = (level[bh] + p_base[bh, row_at, :]) * p_inv[bh, row_at, :]
            dam = p_half[bh, row_at, :] * (1.0 + lax.erf(arg))
            args[g * 2 + bh] = arg
            weight[g * 2 + bh] = dam * p_c0[bh, row_at, :]
            twice = jnp.concatenate([dam, dam], axis=0).astype(BF16)
            columns = pl.ds(pl.multiple_of(g * WIDE + bh * LANES, LANES), LANES)
            for n in range(8):
                spread[n * 16 : (n + 1) * 16, columns] = twice * masks[n]
            return 0

        lax.fori_loop(0, GROUPS, damage, 0, unroll=4)

    sums = lax.dot_general(spread[...], hot[...], NT, preferred_element_type=F32)
    part[0] = sums[:, :LANES].reshape(COUNTIES, HALF, LANES)
    part[1] = sums[:, LANES:].reshape(COUNTIES, HALF, LANES)

    for i in range(1, LINE):
        yy = lax.rem(y + i, LINE)
        send(part.at[0, pl.ds(2 * yy, 2)], got3.at[0, y], s3, r3, at(z, yy, c))
        zz = lax.rem(z + i, LINE)
        send(part.at[1, pl.ds(2 * zz, 2)], got3.at[1, z], s3, r3, at(zz, y, c))
    got3[0, y] = part[0, pl.ds(2 * y, 2)]
    got3[1, z] = part[1, pl.ds(2 * z, 2)]

    def more(first, last):
        def weigh(g, _):
            row_at = pl.ds(g, 1)
            for bh in range(2):
                arg = args[g * 2 + bh]
                step = p_step[bh, row_at, :]
                rest = (1.0 + lax.erf(arg - step)) * p_c1[bh, row_at, :]
                rest = rest + (1.0 + lax.erf(arg - 2.0 * step)) * p_c2[bh, row_at, :]
                weight[g * 2 + bh] = weight[g * 2 + bh] + p_half[bh, row_at, :] * rest
            return 0

        lax.fori_loop(first, last, weigh, 0, unroll=4)

    more(0, 8)
    drain(got3.at[:, pl.ds(0, 7)], r3)

    for th in range(2):
        total = got3[th, 0]
        for n in range(1, LINE):
            total = total + got3[th, n]
        half_sum[th] = total
    for i in range(1, LINE):
        send(half_sum.at[0], got4.at[0, z], s4, r4, at(lax.rem(z + i, LINE), y, c))
        send(half_sum.at[1], got4.at[1, y], s4, r4, at(z, lax.rem(y + i, LINE), c))
    got4[0, z] = half_sum[0]
    got4[1, y] = half_sum[1]
    more(8, 16)
    drain(got4.at[:, pl.ds(0, 7)], r4)

    for th in range(2):
        total = got4[th, 0]
        for n in range(1, LINE):
            total = total + got4[th, n]
        factor = (1.0 + total / (total + HALF_POINT)).reshape(16, LANES)
        surge_own[th] = factor.astype(BF16)
    for i in range(1, LINE):
        send(surge_own.at[0], surge.at[0, y], s5, r5, at(z, lax.rem(y + i, LINE), c))
        send(surge_own.at[1], surge.at[1, z], s5, r5, at(lax.rem(z + i, LINE), y, c))
    surge[0, y] = surge_own[0]
    surge[1, z] = surge_own[1]
    more(16, 24)
    drain(surge.at[:, pl.ds(0, 7)], r5)

    factors = [surge[th].reshape(COUNTIES * HALF, LANES) for th in range(2)]
    both = jnp.concatenate(factors, axis=1)

    def apply(g, total):
        columns = pl.ds(pl.multiple_of(g * WIDE, WIDE), WIDE)
        found = jnp.dot(both, hot[:, columns], preferred_element_type=F32)
        tiles = jnp.concatenate([weight[g * 2], weight[g * 2 + 1]], axis=1)
        return total + found.reshape(COUNTIES, HALF, WIDE) * tiles[None]

    total = lax.fori_loop(0, GROUPS, apply, jnp.zeros((COUNTIES, HALF, WIDE), F32), unroll=2)

    for bh in range(2):
        county = jnp.broadcast_to(b_county[bh], (HALF, LANES))
        loss = jnp.zeros((HALF, LANES), F32)
        for n in range(COUNTIES):
            loss = loss + jnp.where(county == n, total[n, :, bh * LANES : (bh + 1) * LANES], 0.0)
        masks = pair_masks(b_tract[bh] & 15, bh)
        left = loss
        for piece in range(3):
            rounded = left.astype(BF16)
            left = left - rounded.astype(F32)
            twice = jnp.concatenate([rounded.astype(F32)] * 2, axis=0).astype(BF16)
            for n in range(8):
                terms[n * 16 : (n + 1) * 16, piece * WIDE + bh * LANES : piece * WIDE + (bh + 1) * LANES] = (
                    twice * masks[n]
                )

    tract_part[...] = lax.dot_general(dest[...], terms[...], NT, preferred_element_type=F32).reshape(16, LINE, LANES)

    send(tract_part.at[y * 2 + 1 - c], got6.at[c * LINE + y], s6, r6, at(z, y, 1 - c))
    for i in range(1, LINE):
        yy = lax.rem(y + i, LINE)
        for h in range(2):
            send(tract_part.at[yy * 2 + h], got6.at[c * LINE + y], s6, r6, at(z, yy, h))
    got6[c * LINE + y] = tract_part[y * 2 + c]
    drain(got6.at[pl.ds(0, 15)], r6)

    for h in range(2):
        total = got6[h * LINE]
        for n in range(1, LINE):
            total = total + got6[h * LINE + n]
        for n in range(LINE):
            rows[n, h : h + 1, :] = total[n : n + 1]
    for i in range(1, LINE):
        zz = lax.rem(z + i, LINE)
        send(rows.at[zz], got7.at[z], s7, r7, at(zz, y, c))
    got7[z] = rows[z]
    drain(got7.at[pl.ds(0, 7)], r7)
    final = got7[0]
    for n in range(1, LINE):
        final = final + got7[n]

    row[...] = final[0:1] + final[1:2]
    for i in range(1, 4):
        send(row, got8.at[x], s8, r8, {"real": lax.rem(x + i, 4)})
    got8[x] = row[...]

    lane = lax.broadcasted_iota(jnp.int32, (16, LANES), 1)
    where_tract = lane // HALF == lax.broadcasted_iota(jnp.int32, (16, LANES), 0)
    from_lane = lax.broadcasted_iota(jnp.int32, (LANES, 16), 0)
    to_lane = lax.broadcasted_iota(jnp.int32, (LANES, 16), 1)
    result = jnp.zeros((16, 16), F32)
    for h in range(2):
        picked = jnp.where(where_tract, jnp.broadcast_to(final[h : h + 1], (16, LANES)), 0.0)
        put = ((from_lane & (HALF - 1)) + h * HALF == to_lane).astype(F32)
        result = result + jnp.dot(picked, put, precision=HIGHEST, preferred_element_type=F32)
    loss_out[...] = result

    drain(got8.at[pl.ds(0, 3)], r8)
    over = got8[0] + got8[1] + got8[2] + got8[3]
    put = (from_lane // HALF == to_lane).astype(F32)
    avg_out[...] = jnp.dot(over, put, precision=HIGHEST, preferred_element_type=F32) * (1.0 / REALS_ALL)

    drain(got6.at[pl.ds(0, 15)], s1)
    drain(sites.at[:, pl.ds(0, 7)], s2)
    drain(got3.at[:, pl.ds(0, 7)], s3)
    drain(got4.at[:, pl.ds(0, 7)], s4)
    drain(surge.at[:, pl.ds(0, 7)], s5)
    drain(got6.at[pl.ds(0, 15)], s6)
    drain(got7.at[pl.ds(0, 7)], s7)
    drain(got8.at[pl.ds(0, 3)], s8)


def shards(site_ln, site_of, county_of, tract_of, comp_type, comp_qty, amplify, frag_median, frag_step, frag_beta, state_cost):
    vmem = pltpu.VMEM
    i32 = jnp.int32
    dma = pltpu.SemaphoreType.DMA
    scratch = [
        vmem((2, 1, LANES), i32), vmem((2, 1, LANES), i32), vmem((2, 1, LANES), i32),
        vmem((2, GROUPS, LANES), i32), vmem((2, GROUPS, LANES), i32), vmem((2, GROUPS, LANES), F32),
        vmem((2, LANES), F32), vmem((2, LANES), F32), vmem((2, LANES), F32), vmem((3, TYPES), F32),
        vmem((2, LINE, LINE, HALF, LANES), F32),
    ]
    scratch += [vmem((2, GROUPS, LANES), F32)] * 7
    scratch += [
        vmem((TYPES, GROUPS * WIDE), BF16), vmem((LANES, GROUPS * WIDE), BF16),
        vmem((2 * GROUPS, HALF, LANES), F32), vmem((2 * GROUPS, HALF, LANES), F32),
        vmem((2, COUNTIES, HALF, LANES), F32), vmem((2, LINE, 2, HALF, LANES), F32),
        vmem((2, 2, HALF, LANES), F32), vmem((2, LINE, 2, HALF, LANES), F32),
        vmem((2, 16, LANES), BF16), vmem((2, LINE, 16, LANES), BF16),
        vmem((LANES, 3 * WIDE), BF16), vmem((LANES, 3 * WIDE), BF16),
        vmem((16, LINE, LANES), F32), vmem((16, LINE, LANES), F32),
        vmem((LINE, 2, LANES), F32), vmem((LINE, 2, LANES), F32),
        vmem((1, LANES), F32), vmem((4, 1, LANES), F32),
    ]
    scratch += [dma((6,)), dma((4,)), dma((6,)), dma((6,))]
    scratch += [dma, dma((2,)), dma, dma((2, LINE))] + [dma] * 12
    loss, avg = pl.pallas_call(
        kernel,
        out_shape=(jax.ShapeDtypeStruct((16, 16), F32), jax.ShapeDtypeStruct((1, 16), F32)),
        in_specs=[pl.BlockSpec(memory_space=pl.ANY)] * 11,
        out_specs=(pl.BlockSpec(memory_space=pltpu.VMEM),) * 2,
        scratch_shapes=scratch,
        compiler_params=pltpu.CompilerParams(
            collective_id=0, has_side_effects=True, vmem_limit_bytes=40 * 1024 * 1024
        ),
    )(
        site_ln, site_of.reshape(1, LANES), county_of.reshape(1, LANES), tract_of.reshape(1, LANES),
        comp_type, comp_qty, amplify,
        frag_median.reshape(2, LANES), frag_step.reshape(2, LANES), frag_beta.reshape(2, LANES), state_cost,
    )
    return loss, avg.reshape(16)


def solution(mesh):
    in_specs = (
        P("real", "bld"), P("bld"), P("bld"), P("bld"), P(None, "bld"), P(None, "bld"), P(None, "bld"),
        P(), P(), P(), P(),
    )
    out_specs = (P("bld", "real"), P("bld"))
    return jax.shard_map(shards, mesh=mesh, in_specs=in_specs, out_specs=out_specs, check_vma=False)
```

time: 527 us -> 69.9 us (0.13)
  waiting for transfers between devices: 462 us -> 0 us
  Pallas kernels: 0 us -> 62.2 us
  matrix products: 31.7 us -> 0 us
  between operations: 13.8 us -> 0.68 us
  blocking collectives: 8.4 us -> 0 us
    psum x2 -> x0, waiting for transfers between devices: 377 us -> none  [the longest x1 193 us: shards(): lax.psum(jnp.dot(matches, flipped, precision=highest, preferred_element_t...]
    all_gather x1 -> x0, waiting for transfers between devices: 84.3 us -> none  [shards(): block_part = lax.all_gather(site_ln, 'bld', axis=1, tiled=True)]
    pallas_call x0 -> x1, Pallas kernels: none -> 62.2 us  [shards(): pl.pallas_call(kernel, out_shape=(jax.ShapeDtypeStruct((16, 16), F32), ja...]
    dot_general x51 -> x0, matrix products: 31.7 us -> none  [the longest x24 12.2 us: collect(): jnp.dot(group_part, matches, preferred_element_type=jnp.float32)]
    psum x1 -> x0, blocking collectives: 8.4 us -> none  [shards(): tract_sums = lax.psum(jnp.sum(own_tracts, axis=1), 'real')]
    unnamed x8 -> x24, local copies, waits for them, and re-layouts: 0.72 us -> 6.58 us
  transfers between devices with their start and end apart: 3 -> 0, of which waited for: 3 -> 0; matrix products, arithmetic and copies ran while one was open for 1% -> 0% of each run, Pallas kernels for 0% -> 0%
where the time goes in v1:
time: 69.9 us; the launch traced here: 69.4 us
  Pallas kernels  62.2 us (89%)
  local copies, waits for them, and re-layouts  6.58 us (9%)
    pallas_call x1, Pallas kernels, shards(): pl.pallas_call(kernel, out_shape=(jax.ShapeDtypeStruct((16, 16), F32), ja...  62.2 us
    unnamed x24, local copies, waits for them, and re-layouts  6.58 us

profile of v1, /device:TPU:1, one launch (start us, length us, event | category | flops | bytes accessed | tf_op | source)
XLA Modules:
  0.0 69.4 jit_solution(3690008608357190746)
XLA Ops:
  0.6 0.0 copy-start.3
  0.6 0.0 copy-start.6
  0.7 0.0 copy-start.7
  0.7 0.0 copy-start.5
  0.7 0.7 copy-done.3
  1.3 0.0 copy-done.6
  1.3 0.0 copy-done.7
  1.3 0.0 copy-done.5
  1.4 0.0 copy-start
  1.4 0.7 %copy-done = s32[24,128]{1,0:T(8,128)S(1)} copy-done((s32[24,128]{1,0:T(8,128)S(1)}, s32[24,128]{1,0:T(8,128)}, u32[]{:S(2)}) %copy-start) | copy-done | bytes 12312
  2.1 0.0 copy-start.1
  2.1 0.7 %copy-done.1 = s32[24,128]{1,0:T(8,128)S(1)} copy-done((s32[24,128]{1,0:T(8,128)S(1)}, s32[24,128]{1,0:T(8,128)}, u32[]{:S(2)}) %copy-start.1) | copy-done | bytes 12312
  2.8 0.0 copy-start.2
  2.8 0.7 %copy-done.2 = f32[24,128]{1,0:T(8,128)S(1)} copy-done((f32[24,128]{1,0:T(8,128)S(1)}, f32[24,128]{1,0:T(8,128)}, u32[]{:S(2)}) %copy-start.2) | copy-done | bytes 12312
  3.5 0.0 copy-start.4
  3.5 0.7 copy-done.4
  4.2 0.0 copy-start.8
  4.2 0.7 copy-done.8
  4.8 0.0 copy-start.9
  4.8 0.7 copy-done.9
  5.5 0.7 copy-done.10
  6.1 62.2 %shard_map.122 = (f32[16,16]{1,0:T(8,128)S(1)}, f32[1,16]{1,0:T(1,128)S(1)}) custom-call(f32[16,128]{1,0:T(8,128)S(1)} %copy-done.3, s32[1,128]{1,0:T(1,128)S(1)} %bitcast.10, s32[1,128]{1,0:T(1,128)S(1)} %bitcast.11, s32[1,128]{1,0:T(1,128)S(1)} %bitcast.12, s32[24,128]{1,0:T(8,128)S(1)} %copy-done, s32[24,128]{1,0:T(8,128)S(1)} %copy-done.1, ...), custom_call_target="tpu_custom_call" | custom-call | tf_op jit(solution)/shard_map/pallas_call | solution.py:385
  68.3 0.6 copy.15
  68.9 0.5 copy.16
  (1 shorter events, 0.0 us)
Async XLA Ops:
  0.6 0.7 %copy-start.3 = (f32[16,128]{1,0:T(8,128)S(1)}, f32[16,128]{1,0:T(8,128)}, u32[]{:S(2)}) copy-start(f32[16,128]{1,0:T(8,128)} %site_ln.1) | copy-start | bytes 24580
  0.6 0.7 copy-start.6
  0.7 0.7 copy-start.7
  0.7 0.7 %copy-start.5 = (f32[256]{0:T(256)S(1)}, f32[256]{0:T(256)}, u32[]{:S(2)}) copy-start(f32[256]{0:T(256)} %param.18) | copy-start | bytes 3076
  1.4 0.7 %copy-start = (s32[24,128]{1,0:T(8,128)S(1)}, s32[24,128]{1,0:T(8,128)}, u32[]{:S(2)}) copy-start(s32[24,128]{1,0:T(8,128)} %comp_type.1) | copy-start | bytes 36868
  2.1 0.7 %copy-start.1 = (s32[24,128]{1,0:T(8,128)S(1)}, s32[24,128]{1,0:T(8,128)}, u32[]{:S(2)}) copy-start(s32[24,128]{1,0:T(8,128)} %comp_qty.1) | copy-start | bytes 36868
  2.8 0.7 %copy-start.2 = (f32[24,128]{1,0:T(8,128)S(1)}, f32[24,128]{1,0:T(8,128)}, u32[]{:S(2)}) copy-start(f32[24,128]{1,0:T(8,128)} %amplify.1) | copy-start | bytes 36868
  3.5 0.7 copy-start.4
  4.2 0.7 copy-start.8
  4.8 0.7 copy-start.9
  5.5 0.7 copy-start.10

commit v2 on v1

--- a/solution.py
+++ b/solution.py
@@ -20,6 +20,7 @@
 BF16 = jnp.bfloat16
 HIGHEST = lax.Precision.HIGHEST
 NT = (((1,), (1,)), ((), ()))
+FAR_FIRST = (4, 3, 5, 2, 6, 1, 7)
 
 
 def lanes_of(table, index):
@@ -34,12 +35,12 @@
     site_ln, site_of, county_of, tract_of, comp_type, comp_qty, amplify,
     frag_median, frag_step, frag_beta, state_cost,
     loss_out, avg_out,
-    b_site, b_county, b_tract, b_type, b_qty, b_amp,
+    b_ln, b_site, b_county, b_tract, b_type, b_qty, b_amp,
     t_med, t_step, t_beta, t_cost,
     sites, p_base, p_inv, p_step, p_half, p_c0, p_c1, p_c2,
     hot, spread, args, weight,
     part, got3, half_sum, got4, surge_own, surge,
-    dest, terms, tract_part, got6, rows, got7, row, got8,
+    dest, terms, tract_part, got6, rows, got7, joint, got8,
     loc_sem, par_sem, bld_send, bld_recv,
     s1, r1, s2, r2, s3, r3, s4, r4, s5, r5, s6, r6, s7, r7, s8, r8,
 ):
@@ -63,13 +64,13 @@
     def hello(who):
         pl.semaphore_signal(barrier, inc=1, device_id=who, device_id_type=MESH)
 
-    hello(at(z, y, 1 - c))
-    for i in range(1, LINE):
+    for i in FAR_FIRST:
         for h in range(2):
             hello(at(z, lax.rem(y + i, LINE), h))
             hello(at(lax.rem(z + i, LINE), y, h))
-    for i in range(1, 4):
+    for i in (2, 1, 3):
         hello({"real": lax.rem(x + i, 4)})
+    hello(at(z, y, 1 - c))
 
     buildings = (
         (site_of, b_site), (county_of, b_county), (tract_of, b_tract),
@@ -78,26 +79,29 @@
     tables = ((frag_median, t_med), (frag_step, t_step), (frag_beta, t_beta), (state_cost, t_cost))
     own = [pltpu.make_async_copy(a, b.at[0], loc_sem.at[n]) for n, (a, b) in enumerate(buildings)]
     own += [pltpu.make_async_copy(a, b, par_sem.at[n]) for n, (a, b) in enumerate(tables)]
+    own.append(pltpu.make_async_copy(site_ln, b_ln, par_sem.at[4]))
     for copy in own:
         copy.start()
 
     pl.semaphore_wait(barrier, 1 + 4 * (LINE - 1) + 3)
+    for copy in own:
+        copy.wait()
 
     p = y * (1 - c) + z * c
     q = z * (1 - c) + y * c
     mine = sites.at[c, q, p]
-    local = pltpu.make_async_copy(site_ln.at[pl.ds(pl.multiple_of(c * HALF, HALF), HALF)], mine, r1.at[c])
+    local = pltpu.make_async_copy(b_ln.at[pl.ds(pl.multiple_of(c * HALF, HALF), HALF)], mine, r1.at[c])
     local.start()
-    send(site_ln.at[pl.ds(pl.multiple_of((1 - c) * HALF, HALF), HALF)], mine, s1, r1.at[c], at(z, y, 1 - c))
-    for i in range(1, LINE):
+    for i in FAR_FIRST:
         pp = lax.rem(p + i, LINE)
         for h in range(2):
             zz = q * (1 - c) + pp * c
             yy = pp * (1 - c) + q * c
-            send(site_ln.at[pl.ds(h * HALF, HALF)], mine, s1, r1.at[c], at(zz, yy, h))
+            send(b_ln.at[pl.ds(h * HALF, HALF)], mine, s1, r1.at[c], at(zz, yy, h))
+    send(b_ln.at[pl.ds(pl.multiple_of((1 - c) * HALF, HALF), HALF)], mine, s1, r1.at[c], at(z, y, 1 - c))
     trade = [
         pltpu.make_async_remote_copy(
-            src_ref=a, dst_ref=b.at[1], send_sem=bld_send.at[n], recv_sem=bld_recv.at[n],
+            src_ref=b.at[0], dst_ref=b.at[1], send_sem=bld_send.at[n], recv_sem=bld_recv.at[n],
             device_id=at(z, y, 1 - c), device_id_type=MESH,
         )
         for n, (a, b) in enumerate(buildings)
@@ -106,14 +110,12 @@
         copy.start()
 
     drain(sites.at[0, z], r1.at[0])
-    for i in range(1, LINE):
+    for i in FAR_FIRST:
         send(sites.at[0, z], sites.at[0, z], s2, r2.at[0, i], at(lax.rem(z + i, LINE), y, c))
     drain(sites.at[1, y], r1.at[1])
-    for i in range(1, LINE):
+    for i in FAR_FIRST:
         send(sites.at[1, y], sites.at[1, y], s2, r2.at[1, i], at(z, lax.rem(y + i, LINE), c))
 
-    for copy in own:
-        copy.wait()
     for copy in trade:
         copy.wait()
     inv_row = ROOT_HALF / t_beta[...]
@@ -224,7 +226,7 @@
     part[0] = sums[:, :LANES].reshape(COUNTIES, HALF, LANES)
     part[1] = sums[:, LANES:].reshape(COUNTIES, HALF, LANES)
 
-    for i in range(1, LINE):
+    for i in FAR_FIRST:
         yy = lax.rem(y + i, LINE)
         send(part.at[0, pl.ds(2 * yy, 2)], got3.at[0, y], s3, r3, at(z, yy, c))
         zz = lax.rem(z + i, LINE)
@@ -253,7 +255,7 @@
         for n in range(1, LINE):
             total = total + got3[th, n]
         half_sum[th] = total
-    for i in range(1, LINE):
+    for i in FAR_FIRST:
         send(half_sum.at[0], got4.at[0, z], s4, r4, at(lax.rem(z + i, LINE), y, c))
         send(half_sum.at[1], got4.at[1, y], s4, r4, at(z, lax.rem(y + i, LINE), c))
     got4[0, z] = half_sum[0]
@@ -267,7 +269,7 @@
             total = total + got4[th, n]
         factor = (1.0 + total / (total + HALF_POINT)).reshape(16, LANES)
         surge_own[th] = factor.astype(BF16)
-    for i in range(1, LINE):
+    for i in FAR_FIRST:
         send(surge_own.at[0], surge.at[0, y], s5, r5, at(z, lax.rem(y + i, LINE), c))
         send(surge_own.at[1], surge.at[1, z], s5, r5, at(lax.rem(z + i, LINE), y, c))
     surge[0, y] = surge_own[0]
@@ -304,33 +306,39 @@
 
     tract_part[...] = lax.dot_general(dest[...], terms[...], NT, preferred_element_type=F32).reshape(16, LINE, LANES)
 
-    send(tract_part.at[y * 2 + 1 - c], got6.at[c * LINE + y], s6, r6, at(z, y, 1 - c))
-    for i in range(1, LINE):
+    for i in FAR_FIRST:
         yy = lax.rem(y + i, LINE)
         for h in range(2):
             send(tract_part.at[yy * 2 + h], got6.at[c * LINE + y], s6, r6, at(z, yy, h))
+    send(tract_part.at[y * 2 + 1 - c], got6.at[c * LINE + y], s6, r6, at(z, y, 1 - c))
     got6[c * LINE + y] = tract_part[y * 2 + c]
     drain(got6.at[pl.ds(0, 15)], r6)
 
+    halves = []
     for h in range(2):
         total = got6[h * LINE]
         for n in range(1, LINE):
             total = total + got6[h * LINE + n]
+        halves.append(total)
         for n in range(LINE):
             rows[n, h : h + 1, :] = total[n : n + 1]
-    for i in range(1, LINE):
+    total = halves[0] + halves[1]
+    for n in range(LINE):
+        joint[n] = total[n : n + 1]
+    for i, k in ((4, 2), (4, 1), (4, 3), (3, 2), (5, 2), (4, 0), (3, 1), (3, 3), (5, 1), (5, 3), (2, 2), (6, 2), (3, 0), (5, 0),
+                 (2, 1), (2, 3), (6, 1), (6, 3), (1, 2), (7, 2), (2, 0), (6, 0), (1, 1), (1, 3), (7, 1), (7, 3), (0, 2),
+                 (1, 0), (7, 0), (0, 1), (0, 3)):
         zz = lax.rem(z + i, LINE)
-        send(rows.at[zz], got7.at[z], s7, r7, at(zz, y, c))
+        if k == 0:
+            send(rows.at[zz], got7.at[z], s7, r7, at(zz, y, c))
+        else:
+            who = {"bld": (zz * LINE + y) * 2 + c, "real": lax.rem(x + k, 4)}
+            send(joint.at[zz], got8.at[(k - 1) * LINE + z], s8, r8, who)
     got7[z] = rows[z]
     drain(got7.at[pl.ds(0, 7)], r7)
     final = got7[0]
     for n in range(1, LINE):
         final = final + got7[n]
-
-    row[...] = final[0:1] + final[1:2]
-    for i in range(1, 4):
-        send(row, got8.at[x], s8, r8, {"real": lax.rem(x + i, 4)})
-    got8[x] = row[...]
 
     lane = lax.broadcasted_iota(jnp.int32, (16, LANES), 1)
     where_tract = lane // HALF == lax.broadcasted_iota(jnp.int32, (16, LANES), 0)
@@ -343,8 +351,10 @@
         result = result + jnp.dot(picked, put, precision=HIGHEST, preferred_element_type=F32)
     loss_out[...] = result
 
-    drain(got8.at[pl.ds(0, 3)], r8)
-    over = got8[0] + got8[1] + got8[2] + got8[3]
+    drain(got8, r8)
+    over = final[0:1] + final[1:2]
+    for n in range(3 * LINE):
+        over = over + got8[n]
     put = (from_lane // HALF == to_lane).astype(F32)
     avg_out[...] = jnp.dot(over, put, precision=HIGHEST, preferred_element_type=F32) * (1.0 / REALS_ALL)
 
@@ -355,7 +365,7 @@
     drain(surge.at[:, pl.ds(0, 7)], s5)
     drain(got6.at[pl.ds(0, 15)], s6)
     drain(got7.at[pl.ds(0, 7)], s7)
-    drain(got8.at[pl.ds(0, 3)], s8)
+    drain(got8, s8)
 
 
 def shards(site_ln, site_of, county_of, tract_of, comp_type, comp_qty, amplify, frag_median, frag_step, frag_beta, state_cost):
@@ -363,6 +373,7 @@
     i32 = jnp.int32
     dma = pltpu.SemaphoreType.DMA
     scratch = [
+        vmem((2 * HALF, LANES), F32),
         vmem((2, 1, LANES), i32), vmem((2, 1, LANES), i32), vmem((2, 1, LANES), i32),
         vmem((2, GROUPS, LANES), i32), vmem((2, GROUPS, LANES), i32), vmem((2, GROUPS, LANES), F32),
         vmem((2, LANES), F32), vmem((2, LANES), F32), vmem((2, LANES), F32), vmem((3, TYPES), F32),
@@ -378,18 +389,18 @@
         vmem((LANES, 3 * WIDE), BF16), vmem((LANES, 3 * WIDE), BF16),
         vmem((16, LINE, LANES), F32), vmem((16, LINE, LANES), F32),
         vmem((LINE, 2, LANES), F32), vmem((LINE, 2, LANES), F32),
-        vmem((1, LANES), F32), vmem((4, 1, LANES), F32),
+        vmem((LINE, 1, LANES), F32), vmem((3 * LINE, 1, LANES), F32),
     ]
-    scratch += [dma((6,)), dma((4,)), dma((6,)), dma((6,))]
+    scratch += [dma((6,)), dma((5,)), dma((6,)), dma((6,))]
     scratch += [dma, dma((2,)), dma, dma((2, LINE))] + [dma] * 12
     loss, avg = pl.pallas_call(
         kernel,
         out_shape=(jax.ShapeDtypeStruct((16, 16), F32), jax.ShapeDtypeStruct((1, 16), F32)),
-        in_specs=[pl.BlockSpec(memory_space=pl.ANY)] * 11,
+        in_specs=[pl.BlockSpec(memory_space=pltpu.HBM)] * 11,
         out_specs=(pl.BlockSpec(memory_space=pltpu.VMEM),) * 2,
         scratch_shapes=scratch,
         compiler_params=pltpu.CompilerParams(
-            collective_id=0, has_side_effects=True, vmem_limit_bytes=40 * 1024 * 1024
+            collective_id=0, has_side_effects=True, vmem_limit_bytes=56 * 1024 * 1024
         ),
     )(
         site_ln, site_of.reshape(1, LANES), county_of.reshape(1, LANES), tract_of.reshape(1, LANES),

time: 69.9 us -> 61.9 us (0.89)
  local copies, waits for them, and re-layouts: 6.58 us -> 1.81 us
  Pallas kernels: 62.2 us -> 59.3 us
    unnamed x24 -> x4, local copies, waits for them, and re-layouts: 6.58 us -> 1.81 us
    pallas_call x1, Pallas kernels: 62.2 us -> 59.3 us  [shards(): pl.pallas_call(kernel, out_shape=(jax.ShapeDtypeStruct((16, 16), F32), ja...]
where the time goes in v2:
time: 61.9 us; the launch traced here: 61.8 us
  Pallas kernels  59.3 us (96%)
  local copies, waits for them, and re-layouts  1.81 us (3%)
  between operations  0.65 us (1%)
    pallas_call x1, Pallas kernels, shards(): pl.pallas_call(kernel, out_shape=(jax.ShapeDtypeStruct((16, 16), F32), ja...  59.3 us
    unnamed x4, local copies, waits for them, and re-layouts  1.81 us

profile of v2, /device:TPU:1, one launch (start us, length us, event | category | flops | bytes accessed | tf_op | source)
XLA Modules:
  0.0 61.8 jit_solution(2354738859929780690)
XLA Ops:
  0.6 59.3 %shard_map.122 = (f32[16,16]{1,0:T(8,128)}, f32[1,16]{1,0:T(1,128)}) custom-call(f32[16,128]{1,0:T(8,128)} %site_ln.1, s32[1,128]{1,0:T(1,128)} %bitcast.10, s32[1,128]{1,0:T(1,128)} %bitcast.11, s32[1,128]{1,0:T(1,128)} %bitcast.12, s32[24,128]{1,0:T(8,128)} %comp_type.1, s32[24,128]{1,0:T(8,128)} %comp_qty.1, f32[24,128]{1,0:T(8,128)} %amplify.1, ...), custom_call_target="tpu_custom_call" | custom-call | tf_op jit(solution)/shard_map/pallas_call | solution.py:396
  60.0 0.0 copy-start
  60.0 1.3 %copy.15 = f32[16,16]{1,0:T(8,128)} copy(f32[16,16]{1,0:T(8,128)} %get-tuple-element.8) | data formatting | bytes 2048
  61.3 0.0 copy-done
  61.3 0.5 copy.16
Async XLA Ops:
  60.0 1.3 %copy-start = (f32[1,16]{1,0:T(1,128)S(1)}, f32[1,16]{1,0:T(1,128)}, u32[]{:S(2)}) copy-start(f32[1,16]{1,0:T(1,128)} %get-tuple-element.5) | copy-start | bytes 196

commit v3 on v2

--- a/solution.py
+++ b/solution.py
@@ -20,7 +20,10 @@
 BF16 = jnp.bfloat16
 HIGHEST = lax.Precision.HIGHEST
 NT = (((1,), (1,)), ((), ()))
+QUARTER = 4
+STEPS = 65535.0 / 8.0
 FAR_FIRST = (4, 3, 5, 2, 6, 1, 7)
+CHUNK = 4
 
 
 def lanes_of(table, index):
@@ -35,7 +38,7 @@
     site_ln, site_of, county_of, tract_of, comp_type, comp_qty, amplify,
     frag_median, frag_step, frag_beta, state_cost,
     loss_out, avg_out,
-    b_ln, b_site, b_county, b_tract, b_type, b_qty, b_amp,
+    b_ln, packed, b_site, b_county, b_tract, b_type, b_qty, b_amp,
     t_med, t_step, t_beta, t_cost,
     sites, p_base, p_inv, p_step, p_half, p_c0, p_c1, p_c2,
     hot, spread, args, weight,
@@ -83,22 +86,26 @@
     for copy in own:
         copy.start()
 
-    pl.semaphore_wait(barrier, 1 + 4 * (LINE - 1) + 3)
     for copy in own:
         copy.wait()
+    fixed = ((b_ln[...] + 4.0) * STEPS + 0.5).astype(jnp.int32)
+    for h in range(2):
+        first = h * HALF
+        packed[h] = fixed[first : first + QUARTER] | (fixed[first + QUARTER : first + HALF] << 16)
+    pl.semaphore_wait(barrier, 1 + 4 * (LINE - 1) + 3)
 
     p = y * (1 - c) + z * c
     q = z * (1 - c) + y * c
     mine = sites.at[c, q, p]
-    local = pltpu.make_async_copy(b_ln.at[pl.ds(pl.multiple_of(c * HALF, HALF), HALF)], mine, r1.at[c])
+    local = pltpu.make_async_copy(packed.at[c], mine, r1.at[c])
     local.start()
     for i in FAR_FIRST:
         pp = lax.rem(p + i, LINE)
         for h in range(2):
             zz = q * (1 - c) + pp * c
             yy = pp * (1 - c) + q * c
-            send(b_ln.at[pl.ds(h * HALF, HALF)], mine, s1, r1.at[c], at(zz, yy, h))
-    send(b_ln.at[pl.ds(pl.multiple_of((1 - c) * HALF, HALF), HALF)], mine, s1, r1.at[c], at(z, y, 1 - c))
+            send(packed.at[h], mine, s1, r1.at[c], at(zz, yy, h))
+    send(packed.at[1 - c], mine, s1, r1.at[c], at(z, y, 1 - c))
     trade = [
         pltpu.make_async_remote_copy(
             src_ref=b.at[0], dst_ref=b.at[1], send_sem=bld_send.at[n], recv_sem=bld_recv.at[n],
@@ -186,13 +193,17 @@
 
     low = [jnp.broadcast_to(b_site[bh] & (LANES - 1), (HALF, LANES)) for bh in range(2)]
     high = [jnp.broadcast_to(b_site[bh] // LANES, (HALF, LANES)) for bh in range(2)]
-    level = [jnp.zeros((HALF, LANES), F32) for _ in range(2)]
+    second = (lax.broadcasted_iota(jnp.int32, (HALF, LANES), 0) >= QUARTER).astype(jnp.int32)
+    apart = [[high[bh] - second * stride for bh in range(2)] for stride in (2, 16)]
+    level = [jnp.zeros((HALF, LANES), jnp.int32) for _ in range(2)]
 
     def pick(level, route, line):
-        for n in range(LINE):
-            tile = sites[route, line, n]
+        for n in range(0, LINE, 2):
+            tile = jnp.concatenate([sites[route, line, n], sites[route, line, n + 1]], axis=0)
             block = (line * 16 + 2 * n) if route == 0 else (n * 16 + line * 2 + 1)
-            level = [jnp.where(high[bh] == block, lanes_of(tile, low[bh]), level[bh]) for bh in range(2)]
+            level = [
+                jnp.where(apart[route][bh] == block, lanes_of(tile, low[bh]), level[bh]) for bh in range(2)
+            ]
         return level
 
     level = pick(level, 0, z)
@@ -206,23 +217,29 @@
         level = pick(level, 1, yy)
 
     for bh in range(2):
-        masks = pair_masks(b_county[bh], bh)
-
-        def damage(g, _):
-            row_at = pl.ds(g, 1)
-            arg = (level[bh] + p_base[bh, row_at, :]) * p_inv[bh, row_at, :]
-            dam = p_half[bh, row_at, :] * (1.0 + lax.erf(arg))
-            args[g * 2 + bh] = arg
-            weight[g * 2 + bh] = dam * p_c0[bh, row_at, :]
-            twice = jnp.concatenate([dam, dam], axis=0).astype(BF16)
-            columns = pl.ds(pl.multiple_of(g * WIDE + bh * LANES, LANES), LANES)
-            for n in range(8):
-                spread[n * 16 : (n + 1) * 16, columns] = twice * masks[n]
-            return 0
-
-        lax.fori_loop(0, GROUPS, damage, 0, unroll=4)
-
-    sums = lax.dot_general(spread[...], hot[...], NT, preferred_element_type=F32)
+        word = level[bh][:QUARTER] | level[bh][QUARTER:]
+        both_halves = jnp.concatenate([word & 0xFFFF, (word >> 16) & 0xFFFF], axis=0)
+        level[bh] = both_halves.astype(F32) * (1.0 / STEPS) - 4.0
+
+    county_masks = [pair_masks(b_county[bh], bh) for bh in range(2)]
+    sums = None
+    for j in range(GROUPS // CHUNK + 1):
+        if j < GROUPS // CHUNK:
+            for g in range(j * CHUNK, (j + 1) * CHUNK):
+                for bh in range(2):
+                    arg = (level[bh] + p_base[bh, g : g + 1, :]) * p_inv[bh, g : g + 1, :]
+                    dam = p_half[bh, g : g + 1, :] * (1.0 + lax.erf(arg))
+                    args[g * 2 + bh] = arg
+                    weight[g * 2 + bh] = dam * p_c0[bh, g : g + 1, :]
+                    twice = jnp.concatenate([dam, dam], axis=0).astype(BF16)
+                    first = g * WIDE + bh * LANES
+                    for n in range(8):
+                        spread[n * 16 : (n + 1) * 16, first : first + LANES] = twice * county_masks[bh][n]
+        if j:
+            columns = slice((j - 1) * CHUNK * WIDE, j * CHUNK * WIDE)
+            found = lax.dot_general(spread[:, columns], hot[:, columns], NT, preferred_element_type=F32)
+            sums = found if sums is None else sums + found
+
     part[0] = sums[:, :LANES].reshape(COUNTIES, HALF, LANES)
     part[1] = sums[:, LANES:].reshape(COUNTIES, HALF, LANES)
 
@@ -286,7 +303,7 @@
         tiles = jnp.concatenate([weight[g * 2], weight[g * 2 + 1]], axis=1)
         return total + found.reshape(COUNTIES, HALF, WIDE) * tiles[None]
 
-    total = lax.fori_loop(0, GROUPS, apply, jnp.zeros((COUNTIES, HALF, WIDE), F32), unroll=2)
+    total = lax.fori_loop(0, GROUPS, apply, jnp.zeros((COUNTIES, HALF, WIDE), F32), unroll=8)
 
     for bh in range(2):
         county = jnp.broadcast_to(b_county[bh], (HALF, LANES))
@@ -358,7 +375,7 @@
     put = (from_lane // HALF == to_lane).astype(F32)
     avg_out[...] = jnp.dot(over, put, precision=HIGHEST, preferred_element_type=F32) * (1.0 / REALS_ALL)
 
-    drain(got6.at[pl.ds(0, 15)], s1)
+    drain(sites.at[0, pl.ds(0, 3), pl.ds(0, 5)], s1)
     drain(sites.at[:, pl.ds(0, 7)], s2)
     drain(got3.at[:, pl.ds(0, 7)], s3)
     drain(got4.at[:, pl.ds(0, 7)], s4)
@@ -373,11 +390,11 @@
     i32 = jnp.int32
     dma = pltpu.SemaphoreType.DMA
     scratch = [
-        vmem((2 * HALF, LANES), F32),
+        vmem((2 * HALF, LANES), F32), vmem((2, QUARTER, LANES), i32),
         vmem((2, 1, LANES), i32), vmem((2, 1, LANES), i32), vmem((2, 1, LANES), i32),
         vmem((2, GROUPS, LANES), i32), vmem((2, GROUPS, LANES), i32), vmem((2, GROUPS, LANES), F32),
         vmem((2, LANES), F32), vmem((2, LANES), F32), vmem((2, LANES), F32), vmem((3, TYPES), F32),
-        vmem((2, LINE, LINE, HALF, LANES), F32),
+        vmem((2, LINE, LINE, QUARTER, LANES), i32),
     ]
     scratch += [vmem((2, GROUPS, LANES), F32)] * 7
     scratch += [

time: 61.9 us -> 57.2 us (0.924)
  Pallas kernels: 59.3 us -> 54.5 us
    pallas_call x1, Pallas kernels: 59.3 us -> 54.5 us  [shards(): pl.pallas_call(kernel, out_shape=(jax.ShapeDtypeStruct((16, 16), F32), ja...]
where the time goes in v3:
time: 57.2 us; the launch traced here: 56.9 us
  Pallas kernels  54.5 us (95%)
  local copies, waits for them, and re-layouts  1.81 us (3%)
  between operations  0.65 us (1%)
    pallas_call x1, Pallas kernels, shards(): pl.pallas_call(kernel, out_shape=(jax.ShapeDtypeStruct((16, 16), F32), ja...  54.5 us
    unnamed x4, local copies, waits for them, and re-layouts  1.81 us

profile of v3, /device:TPU:1, one launch (start us, length us, event | category | flops | bytes accessed | tf_op | source)
XLA Modules:
  0.0 56.9 jit_solution(970211119361340801)
XLA Ops:
  0.6 54.5 %shard_map.122 = (f32[16,16]{1,0:T(8,128)}, f32[1,16]{1,0:T(1,128)}) custom-call(f32[16,128]{1,0:T(8,128)} %site_ln.1, s32[1,128]{1,0:T(1,128)} %bitcast.10, s32[1,128]{1,0:T(1,128)} %bitcast.11, s32[1,128]{1,0:T(1,128)} %bitcast.12, s32[24,128]{1,0:T(8,128)} %comp_type.1, s32[24,128]{1,0:T(8,128)} %comp_qty.1, f32[24,128]{1,0:T(8,128)} %amplify.1, ...), custom_call_target="tpu_custom_call" | custom-call | tf_op jit(solution)/shard_map/pallas_call | solution.py:413
  55.1 0.0 copy-start
  55.1 1.3 %copy.15 = f32[16,16]{1,0:T(8,128)} copy(f32[16,16]{1,0:T(8,128)} %get-tuple-element.8) | data formatting | bytes 2048
  56.4 0.0 copy-done
  56.4 0.5 copy.16
Async XLA Ops:
  55.1 1.3 %copy-start = (f32[1,16]{1,0:T(1,128)S(1)}, f32[1,16]{1,0:T(1,128)}, u32[]{:S(2)}) copy-start(f32[1,16]{1,0:T(1,128)} %get-tuple-element.5) | copy-start | bytes 196

commit v4 on v3

--- a/solution.py
+++ b/solution.py
@@ -369,11 +369,14 @@
     loss_out[...] = result
 
     drain(got8, r8)
-    over = final[0:1] + final[1:2]
-    for n in range(3 * LINE):
-        over = over + got8[n]
-    put = (from_lane // HALF == to_lane).astype(F32)
-    avg_out[...] = jnp.dot(over, put, precision=HIGHEST, preferred_element_type=F32) * (1.0 / REALS_ALL)
+    over = [final[0:1] + final[1:2]] + [got8[n] for n in range(3 * LINE)]
+    while len(over) > 1:
+        over = [sum(over[n : n + 2]) for n in range(0, len(over), 2)]
+    over = jnp.broadcast_to(over[0], (HALF, LANES))
+    for shift in (1, 2, 4):
+        over = over + pltpu.roll(over, LANES - shift, 1)
+    index = (lax.broadcasted_iota(jnp.int32, (HALF, LANES), 1) * HALF) & (LANES - 1)
+    avg_out[...] = lanes_of(over, index)[0:1, 0:16] * (1.0 / REALS_ALL)
 
     drain(sites.at[0, pl.ds(0, 3), pl.ds(0, 5)], s1)
     drain(sites.at[:, pl.ds(0, 7)], s2)
@@ -412,7 +415,7 @@
     scratch += [dma, dma((2,)), dma, dma((2, LINE))] + [dma] * 12
     loss, avg = pl.pallas_call(
         kernel,
-        out_shape=(jax.ShapeDtypeStruct((16, 16), F32), jax.ShapeDtypeStruct((1, 16), F32)),
+        out_shape=(pltpu.VMEM((16, 16), F32), pltpu.VMEM((1, 16), F32)),
         in_specs=[pl.BlockSpec(memory_space=pltpu.HBM)] * 11,
         out_specs=(pl.BlockSpec(memory_space=pltpu.VMEM),) * 2,
         scratch_shapes=scratch,

time: 57.2 us -> 55.8 us (0.976)
  local copies, waits for them, and re-layouts: 1.81 us -> 1.11 us
  Pallas kernels: 54.5 us -> 53.9 us
    unnamed x4 -> x2, local copies, waits for them, and re-layouts: 1.81 us -> 1.11 us
where the time goes in v4:
time: 55.8 us; the launch traced here: 55.7 us
  Pallas kernels  53.9 us (97%)
  local copies, waits for them, and re-layouts  1.11 us (2%)
  between operations  0.64 us (1%)
    pallas_call x1, Pallas kernels, shards(): pl.pallas_call(kernel, out_shape=(pltpu.VMEM((16, 16), F32), pltpu.VMEM((...  53.9 us

profile of v4, /device:TPU:1, one launch (start us, length us, event | category | flops | bytes accessed | tf_op | source)
XLA Modules:
  0.0 55.7 jit_solution(10392040077440712607)
XLA Ops:
  0.6 53.9 %shard_map.122 = (f32[16,16]{1,0:T(8,128)S(1)}, f32[1,16]{1,0:T(1,128)S(1)}) custom-call(f32[16,128]{1,0:T(8,128)} %site_ln.1, s32[1,128]{1,0:T(1,128)} %bitcast.11, s32[1,128]{1,0:T(1,128)} %bitcast.12, s32[1,128]{1,0:T(1,128)} %bitcast.13, s32[24,128]{1,0:T(8,128)} %comp_type.1, s32[24,128]{1,0:T(8,128)} %comp_qty.1, f32[24,128]{1,0:T(8,128)} %amplify.1, ...), custom_call_target="tpu_custom_call" | custom-call | tf_op jit(solution)/shard_map/pallas_call | solution.py:416
  54.6 0.6 %copy.15 = f32[16,16]{1,0:T(8,128)} copy(f32[16,16]{1,0:T(8,128)S(1)} %get-tuple-element.6) | data formatting | bytes 2048
  55.2 0.5 copy.16

commit v5 on v4

--- a/solution.py
+++ b/solution.py
@@ -40,8 +40,8 @@
     loss_out, avg_out,
     b_ln, packed, b_site, b_county, b_tract, b_type, b_qty, b_amp,
     t_med, t_step, t_beta, t_cost,
-    sites, p_base, p_inv, p_step, p_half, p_c0, p_c1, p_c2,
-    hot, spread, args, weight,
+    line, spare, sites, p_base, p_inv, p_step, p_half, p_c0, p_c1, p_c2,
+    hot, hot_t, spread, args, weight,
     part, got3, half_sum, got4, surge_own, surge,
     dest, terms, tract_part, got6, rows, got7, joint, got8,
     loc_sem, par_sem, bld_send, bld_recv,
@@ -96,7 +96,7 @@
 
     p = y * (1 - c) + z * c
     q = z * (1 - c) + y * c
-    mine = sites.at[c, q, p]
+    mine = line.at[c, p]
     local = pltpu.make_async_copy(packed.at[c], mine, r1.at[c])
     local.start()
     for i in FAR_FIRST:
@@ -116,10 +116,15 @@
     for copy in trade:
         copy.start()
 
-    drain(sites.at[0, z], r1.at[0])
+    def pairs(route, own_line):
+        drain(line.at[route], r1.at[route])
+        for n in range(LINE // 2):
+            sites[route, own_line, n] = jnp.concatenate([line[route, 2 * n], line[route, 2 * n + 1]], axis=0)
+
+    pairs(0, z)
     for i in FAR_FIRST:
         send(sites.at[0, z], sites.at[0, z], s2, r2.at[0, i], at(lax.rem(z + i, LINE), y, c))
-    drain(sites.at[1, y], r1.at[1])
+    pairs(1, y)
     for i in FAR_FIRST:
         send(sites.at[1, y], sites.at[1, y], s2, r2.at[1, i], at(z, lax.rem(y + i, LINE), c))
 
@@ -171,6 +176,8 @@
             columns = pl.ds(pl.multiple_of(g * WIDE + bh * LANES, LANES), LANES)
             for n in range(TYPES // 16):
                 hot[n * 16 : (n + 1) * 16, columns] = jnp.where(types == counts[n], one, zero)
+        columns = pl.ds(pl.multiple_of(g * WIDE, WIDE), WIDE)
+        hot_t[columns, :] = hot[:, columns].T
         return 0
 
     lax.fori_loop(0, GROUPS, make_hot, 0)
@@ -197,10 +204,10 @@
     apart = [[high[bh] - second * stride for bh in range(2)] for stride in (2, 16)]
     level = [jnp.zeros((HALF, LANES), jnp.int32) for _ in range(2)]
 
-    def pick(level, route, line):
+    def pick(level, route, other):
         for n in range(0, LINE, 2):
-            tile = jnp.concatenate([sites[route, line, n], sites[route, line, n + 1]], axis=0)
-            block = (line * 16 + 2 * n) if route == 0 else (n * 16 + line * 2 + 1)
+            tile = sites[route, other, n // 2]
+            block = (other * 16 + 2 * n) if route == 0 else (n * 16 + other * 2 + 1)
             level = [
                 jnp.where(apart[route][bh] == block, lanes_of(tile, low[bh]), level[bh]) for bh in range(2)
             ]
@@ -237,7 +244,7 @@
                         spread[n * 16 : (n + 1) * 16, first : first + LANES] = twice * county_masks[bh][n]
         if j:
             columns = slice((j - 1) * CHUNK * WIDE, j * CHUNK * WIDE)
-            found = lax.dot_general(spread[:, columns], hot[:, columns], NT, preferred_element_type=F32)
+            found = jnp.dot(spread[:, columns], hot_t[columns, :], preferred_element_type=F32)
             sums = found if sums is None else sums + found
 
     part[0] = sums[:, :LANES].reshape(COUNTIES, HALF, LANES)
@@ -378,7 +385,7 @@
     index = (lax.broadcasted_iota(jnp.int32, (HALF, LANES), 1) * HALF) & (LANES - 1)
     avg_out[...] = lanes_of(over, index)[0:1, 0:16] * (1.0 / REALS_ALL)
 
-    drain(sites.at[0, pl.ds(0, 3), pl.ds(0, 5)], s1)
+    drain(spare, s1)
     drain(sites.at[:, pl.ds(0, 7)], s2)
     drain(got3.at[:, pl.ds(0, 7)], s3)
     drain(got4.at[:, pl.ds(0, 7)], s4)
@@ -397,11 +404,11 @@
         vmem((2, 1, LANES), i32), vmem((2, 1, LANES), i32), vmem((2, 1, LANES), i32),
         vmem((2, GROUPS, LANES), i32), vmem((2, GROUPS, LANES), i32), vmem((2, GROUPS, LANES), F32),
         vmem((2, LANES), F32), vmem((2, LANES), F32), vmem((2, LANES), F32), vmem((3, TYPES), F32),
-        vmem((2, LINE, LINE, QUARTER, LANES), i32),
+        vmem((2, LINE, QUARTER, LANES), i32), vmem((15, QUARTER, LANES), i32), vmem((2, LINE, LINE // 2, HALF, LANES), i32),
     ]
     scratch += [vmem((2, GROUPS, LANES), F32)] * 7
     scratch += [
-        vmem((TYPES, GROUPS * WIDE), BF16), vmem((LANES, GROUPS * WIDE), BF16),
+        vmem((TYPES, GROUPS * WIDE), BF16), vmem((GROUPS * WIDE, TYPES), BF16), vmem((LANES, GROUPS * WIDE), BF16),
         vmem((2 * GROUPS, HALF, LANES), F32), vmem((2 * GROUPS, HALF, LANES), F32),
         vmem((2, COUNTIES, HALF, LANES), F32), vmem((2, LINE, 2, HALF, LANES), F32),
         vmem((2, 2, HALF, LANES), F32), vmem((2, LINE, 2, HALF, LANES), F32),

time: 55.8 us -> 55.3 us (level)
  no operation moved by 1% of the time
where the time goes in v5:
time: 55.3 us; the launch traced here: 55.2 us
  Pallas kernels  53.4 us (97%)
  local copies, waits for them, and re-layouts  1.11 us (2%)
  between operations  0.64 us (1%)
    pallas_call x1, Pallas kernels, shards(): pl.pallas_call(kernel, out_shape=(pltpu.VMEM((16, 16), F32), pltpu.VMEM((...  53.4 us
    unnamed x2, local copies, waits for them, and re-layouts  1.11 us

profile of v5, /device:TPU:1, one launch (start us, length us, event | category | flops | bytes accessed | tf_op | source)
XLA Modules:
  0.0 55.2 jit_solution(16599957591561360921)
XLA Ops:
  0.6 53.4 %shard_map.122 = (f32[16,16]{1,0:T(8,128)S(1)}, f32[1,16]{1,0:T(1,128)S(1)}) custom-call(f32[16,128]{1,0:T(8,128)} %site_ln.1, s32[1,128]{1,0:T(1,128)} %bitcast.11, s32[1,128]{1,0:T(1,128)} %bitcast.12, s32[1,128]{1,0:T(1,128)} %bitcast.13, s32[24,128]{1,0:T(8,128)} %comp_type.1, s32[24,128]{1,0:T(8,128)} %comp_qty.1, f32[24,128]{1,0:T(8,128)} %amplify.1, ...), custom_call_target="tpu_custom_call" | custom-call | tf_op jit(solution)/shard_map/pallas_call | solution.py:423
  54.0 0.6 %copy.15 = f32[16,16]{1,0:T(8,128)} copy(f32[16,16]{1,0:T(8,128)S(1)} %get-tuple-element.6) | data formatting | bytes 2048
  54.7 0.5 copy.16
